TPU v7x, 256 devices: a whole 4x4x8 slice. The times are simulated.
256 devices in a mesh: ctx: 64 (over x, y, z_lo, core), ch: 4 (over z_hi).
Axes of the slice: x: 4, y: 4, z: 8 (z_hi: 4, z_lo: 2; z = z_hi * 2 + z_lo), core: 2. Of those that a mesh axis runs over, the one named last changes fastest.
Arguments:
- tokens: bfloat16 [8192, 8192], P('ctx', 'ch'), may hold values from -6 to 6
- value_weight: bfloat16 [8192, 2048], P('ctx', 'ch'), may hold values from -0.0625 to 0.0625
- gate_stream: bfloat16 [8192, 2048], P('ctx', 'ch'), may hold values from -6 to 6
- decay_rate: float32 [16, 2048], P(None, 'ch'), may hold values from 0.5 to 800
- frequency: float32 [16, 2048], P(None, 'ch'), may hold values from 0 to 0.2
- residue: float32 [16, 2048], P(None, 'ch'), may hold values from -2.5 to 2.5
- skip_gain: float32 [2048], P('ch'), may hold values from -4 to 4
- out_weight: bfloat16 [2048, 8192], P(None, 'ch'), may hold values from -0.125 to 0.125
Outputs:
- output: bfloat16 [8192, 8192], P('ctx', 'ch')
All inputs are finite; a program needn't handle non-finite values.
Results may differ from a plain program's by a relative error of at most 0.015.
Values may be sent and summed in bfloat16 or wider, within the bound.
A program may use at most 64 MiB of HBM per device.

v0:
```python
import math

import jax
import jax.numpy as jnp
from jax import lax
from jax.sharding import PartitionSpec as P

exact_mode = lax.Precision.HIGHEST


def modal_filter(times, decay_rate, frequency, residue, length):
    mode_rates = decay_rate / length
    mode_amps = residue * jnp.sqrt(2.0 * mode_rates)

    def add_mode(totals, mode_row):
        one_rate, one_freq, one_amp = mode_row
        term = (
            one_amp[None, :]
            * jnp.exp(-one_rate[None, :] * times[:, None])
            * jnp.cos(one_freq[None, :] * times[:, None])
        )
        return (totals + term, None)

    start_total = jnp.zeros((times.shape[0], residue.shape[1]), jnp.float32)
    totals, _ = lax.scan(add_mode, start_total, (mode_rates, frequency, mode_amps))
    return totals


def make_tables(shards, block_rows, column_group, group_rows, padded_len):
    freq_index = jnp.arange(2 * shards, dtype=jnp.int32)
    source_index = jnp.arange(shards, dtype=jnp.int32)
    angle_outer = (freq_index[:, None] * source_index[None, :] % (2 * shards)).astype(
        jnp.float32
    ) * (math.pi / shards)
    row_index = jnp.arange(block_rows, dtype=jnp.int32)
    angle_inner = (row_index[:, None] * row_index[None, :] % block_rows).astype(jnp.float32) * (
        2.0 * math.pi / block_rows
    )
    global_rows = column_group * group_rows + jnp.arange(group_rows, dtype=jnp.int32)
    angle_twist = (freq_index[:, None] * global_rows[None, :] % padded_len).astype(jnp.float32) * (
        -2.0 * math.pi / padded_len
    )
    return (
        jnp.cos(angle_outer),
        jnp.sin(angle_outer),
        jnp.cos(angle_inner),
        jnp.sin(angle_inner),
        jnp.cos(angle_twist),
        jnp.sin(angle_twist),
    )


def forward_columns(block, cos_outer, sin_outer, twist_cos, twist_sin):
    real_part = jnp.einsum("ka,ajc->kjc", cos_outer, block, precision=exact_mode)
    imag_part = -jnp.einsum("ka,ajc->kjc", sin_outer, block, precision=exact_mode)
    turned_real = real_part * twist_cos[:, :, None] - imag_part * twist_sin[:, :, None]
    turned_imag = real_part * twist_sin[:, :, None] + imag_part * twist_cos[:, :, None]
    return jnp.stack([turned_real, turned_imag])


def along_rows(spectrum, cos_inner, sin_inner):
    real_part = jnp.einsum(
        "kj,rjc->rkc", cos_inner, spectrum[0], precision=exact_mode
    ) + jnp.einsum("kj,rjc->rkc", sin_inner, spectrum[1], precision=exact_mode)
    imag_part = jnp.einsum(
        "kj,rjc->rkc", cos_inner, spectrum[1], precision=exact_mode
    ) - jnp.einsum("kj,rjc->rkc", sin_inner, spectrum[0], precision=exact_mode)
    return (real_part, imag_part)


def on_device(
    tokens, value_weight, gate_stream, decay_rate, frequency, residue, skip_gain, out_weight
):
    whole = lax.all_gather(tokens, "ch", axis=1, tiled=True)
    block_rows = whole.shape[0]
    channels = value_weight.shape[1]
    value = jnp.dot(
        whole,
        lax.all_gather(value_weight, "ctx", axis=0, tiled=True),
        preferred_element_type=jnp.float32,
    ).astype(jnp.bfloat16)
    shards = lax.axis_size("ctx")
    column_group = lax.axis_index("ctx")
    group_rows = block_rows // shards
    length = block_rows * shards
    padded_len = 2 * length
    cos_outer, sin_outer, cos_inner, sin_inner, twist_cos, twist_sin = make_tables(
        shards, block_rows, column_group, group_rows, padded_len
    )
    times = (column_group * block_rows + jnp.arange(block_rows, dtype=jnp.int32)).astype(
        jnp.float32
    )
    kernel = modal_filter(times, decay_rate, frequency, residue, float(length))
    moved_value, moved_kernel = (
        lax.all_to_all(
            value.astype(jnp.float32).reshape(shards, group_rows, channels),
            "ctx",
            split_axis=0,
            concat_axis=0,
            tiled=True,
        ),
        lax.all_to_all(
            kernel.reshape(shards, group_rows, channels),
            "ctx",
            split_axis=0,
            concat_axis=0,
            tiled=True,
        ),
    )
    spread_value, spread_kernel = (
        lax.all_to_all(
            forward_columns(moved_value, cos_outer, sin_outer, twist_cos, twist_sin),
            "ctx",
            split_axis=1,
            concat_axis=2,
            tiled=True,
        ),
        lax.all_to_all(
            forward_columns(moved_kernel, cos_outer, sin_outer, twist_cos, twist_sin),
            "ctx",
            split_axis=1,
            concat_axis=2,
            tiled=True,
        ),
    )
    value_real, value_imag = along_rows(spread_value, cos_inner, sin_inner)
    kernel_real, kernel_imag = along_rows(spread_kernel, cos_inner, sin_inner)
    prod_real = value_real * kernel_real - value_imag * kernel_imag
    prod_imag = value_real * kernel_imag + value_imag * kernel_real
    back_real = jnp.einsum("kj,rkc->rjc", cos_inner, prod_real, precision=exact_mode) - jnp.einsum(
        "kj,rkc->rjc", sin_inner, prod_imag, precision=exact_mode
    )
    back_imag = jnp.einsum("kj,rkc->rjc", cos_inner, prod_imag, precision=exact_mode) + jnp.einsum(
        "kj,rkc->rjc", sin_inner, prod_real, precision=exact_mode
    )
    returned = lax.all_to_all(
        jnp.stack([back_real, back_imag]), "ctx", split_axis=2, concat_axis=1, tiled=True
    )
    untwist_real = returned[0] * twist_cos[:, :, None] + returned[1] * twist_sin[:, :, None]
    untwist_imag = returned[1] * twist_cos[:, :, None] - returned[0] * twist_sin[:, :, None]
    column_rows = (
        jnp.einsum("ka,kjc->ajc", cos_outer, untwist_real, precision=exact_mode)
        - jnp.einsum("ka,kjc->ajc", sin_outer, untwist_imag, precision=exact_mode)
    ) * (1.0 / padded_len)
    conv = lax.all_to_all(column_rows, "ctx", split_axis=0, concat_axis=0, tiled=True).reshape(
        block_rows, channels
    )
    mixed = (
        gate_stream.astype(jnp.float32) * (conv + skip_gain[None, :] * value.astype(jnp.float32))
    ).astype(jnp.bfloat16)
    output = jnp.dot(
        lax.all_gather(mixed, "ch", axis=1, tiled=True),
        out_weight,
        preferred_element_type=jnp.float32,
    )
    return output.astype(jnp.bfloat16)


def solution(mesh):
    placed = (
        P("ctx", "ch"),
        P("ctx", "ch"),
        P("ctx", "ch"),
        P(None, "ch"),
        P(None, "ch"),
        P(None, "ch"),
        P("ch"),
        P(None, "ch"),
    )
    return jax.shard_map(
        on_device, mesh=mesh, in_specs=placed, out_specs=P("ctx", "ch"), check_vma=False
    )
```

profile of v0, /device:TPU:1, one launch (start us, length us, event | category | flops | bytes accessed | tf_op | source)
XLA Modules:
  0.0 331.2 jit_solution(971713384195277510)
XLA Ops:
  8.8 28.2 %while.11 = (s32[]{:T(128)}, f32[128,512]{1,0:T(8,128)S(1)}, f32[16,512]{1,0:T(8,128)S(1)}, f32[16,512]{1,0:T(8,128)S(1)}, f32[16,512]{1,0:T(8,128)}, /*index=5*/s32[]{:T(128)}, s32[]{:T(128)}, s32[]{:T(128)}) while((s32[]{:T(128)}, f32[128,512]{1,0:T(8,128)S(1)}, f32[16,512]{1,0:T(8,128)S(1)}, f32[16,512]{1,0:T(8,128)S(1)}, ...), condition=%wide.region_1.2_spmd.clone, body=%wide.region_0.1_spmd.clone.sunk | while | flops 393987 | bytes 543859 | solution.py:25
  9.6 1.0 select_add_fusion.2
  11.4 1.0 select_add_fusion.2
  13.1 1.0 select_add_fusion.2
  14.9 1.0 select_add_fusion.2
  16.6 1.0 select_add_fusion.2
  18.4 1.0 select_add_fusion.2
  37.8 10.3 %all-to-all-start.2 = ((f32[64,2,512]{2,1,0:T(2,128)}), f32[64,2,512]{2,1,0:T(2,128)S(1)}, u32[]{:S(2)}, u32[]{:S(2)}) async-start(f32[64,2,512]{2,1,0:T(2,128)} %reshape.79), calls=%async_computation.2 | async-start | bytes 524288 | tf_op jit(solution)/shard_map/all_to_all | solution.py:102
  48.2 19.3 %all-gather.3.cloned.1.call-done = bf16[128,8192]{1,0:T(8,128)(2,1)} async-done(((bf16[128,2048]{1,0:T(8,128)(2,1)}), bf16[128,8192]{1,0:T(8,128)(2,1)}) %all-gather.3.cloned.1.call-update) | async-done | bytes 2097168 | tf_op jit(solution)/shard_map/all_gather | solution.py:74
  67.5 114.1 %all-gather.5.cloned.1.call-done = bf16[8192,512]{1,0:T(8,128)(2,1)} async-done(((bf16[128,512]{1,0:T(8,128)(2,1)}), bf16[8192,512]{1,0:T(8,128)(2,1)}) %all-gather.5.cloned.1.call-update) | async-done | bytes 8388624 | tf_op jit(solution)/shard_map/all_gather | solution.py:79
  181.5 5.3 %fusion.5 = f32[128,512]{1,0:T(8,128)S(1)} fusion(bf16[128,8192]{1,0:T(8,128)(2,1)} %all-gather.3.cloned.1.call-done, bf16[8192,512]{1,0:T(8,128)(2,1)} %all-gather.5.cloned.1.call-done), kind=kOutput, calls=%fused_computation.20 | convolution fusion | flops 1073872896 | bytes 10747904 | tf_op jit(solution)/shard_map/dot_general | solution.py:77
  187.7 6.2 %all-to-all-start = ((f32[64,2,512]{2,1,0:T(2,128)}), f32[64,2,512]{2,1,0:T(2,128)S(1)}, u32[]{:S(2)}, u32[]{:S(2)}) async-start(f32[64,2,512]{2,1,0:T(2,128)} %reshape.78), calls=%async_computation | async-start | bytes 524288 | tf_op jit(solution)/shard_map/all_to_all | solution.py:95
  195.5 8.4 %all-to-all-done = f32[64,2,512]{2,1,0:T(2,128)S(1)} async-done(((f32[64,2,512]{2,1,0:T(2,128)}), f32[64,2,512]{2,1,0:T(2,128)S(1)}, u32[]{:S(2)}, u32[]{:S(2)}) %all-to-all-start) | async-done | bytes 262176 | tf_op jit(solution)/shard_map/all_to_all | solution.py:95
  205.6 1.8 copy.40
  207.4 4.5 %all-to-all-start.3 = ((f32[2,128,2,512]{3,2,0,1:T(2,128)}), f32[2,128,2,512]{3,2,0,1:T(2,128)S(1)}, u32[]{:S(2)}, u32[]{:S(2)}) async-start(f32[2,128,2,512]{3,2,0,1:T(2,128)} %copy.40), calls=%async_computation.3 | async-start | bytes 2097152 | tf_op jit(solution)/shard_map/all_to_all | solution.py:118
  212.1 1.8 copy.34
  213.8 16.6 %all-to-all-done.3 = f32[2,128,2,512]{3,2,0,1:T(2,128)S(1)} async-done(((f32[2,128,2,512]{3,2,0,1:T(2,128)}), f32[2,128,2,512]{3,2,0,1:T(2,128)S(1)}, u32[]{:S(2)}, u32[]{:S(2)}) %all-to-all-start.3) | async-done | bytes 1048608 | tf_op jit(solution)/shard_map/all_to_all | solution.py:118
  230.4 4.8 %all-to-all-start.1 = ((f32[2,128,2,512]{3,2,0,1:T(2,128)}), f32[2,128,2,512]{3,2,0,1:T(2,128)S(1)}, u32[]{:S(2)}, u32[]{:S(2)}) async-start(f32[2,128,2,512]{3,2,0,1:T(2,128)} %copy.34), calls=%async_computation.1 | async-start | bytes 2097152 | tf_op jit(solution)/shard_map/all_to_all | solution.py:111
  240.0 13.5 %all-to-all-done.1 = f32[2,128,2,512]{3,2,0,1:T(2,128)S(1)} async-done(((f32[2,128,2,512]{3,2,0,1:T(2,128)}), f32[2,128,2,512]{3,2,0,1:T(2,128)S(1)}, u32[]{:S(2)}, u32[]{:S(2)}) %all-to-all-start.1) | async-done | bytes 1048608 | tf_op jit(solution)/shard_map/all_to_all | solution.py:111
  260.7 1.0 fusion.2
  262.5 22.4 %all_to_all.60 = f32[2,2,128,512]{3,1,0,2:T(2,128)S(1)} all-to-all(f32[2,2,128,512]{3,1,0,2:T(2,128)S(1)} %copy.48), channel_id=1, replica_groups=mesh['ctx'=64,'ch'=4] {'ctx'}, dimensions={2} | all-to-all | bytes 2097152 | tf_op jit(solution)/shard_map/all_to_all | solution.py:136
  287.9 14.1 %all_to_all.61 = f32[64,2,512]{2,1,0:T(2,128)S(1)} all-to-all(f32[64,2,512]{2,1,0:T(2,128)S(1)} %copy.52), channel_id=1, replica_groups=mesh['ctx'=64,'ch'=4] {'ctx'}, dimensions={0} | all-to-all | bytes 524288 | tf_op jit(solution)/shard_map/all_to_all | solution.py:145
  302.3 16.6 %all_gather.11 = bf16[128,2048]{1,0:T(8,128)(2,1)S(1)} all-gather(bf16[128,512]{1,0:T(8,128)(2,1)S(1)} %multiply_convert_fusion), channel_id=1, replica_groups=mesh['ctx'=64,'ch'=4] {'ch'}, dimensions={1}, use_global_device_ids=true | all-gather | bytes 655360 | tf_op jit(solution)/shard_map/all_gather | solution.py:152
  318.9 5.5 %convolution_convert_fusion = bf16[128,2048]{1,0:T(8,128)(2,1)} fusion(bf16[128,2048]{1,0:T(8,128)(2,1)S(1)} %all_gather.11, bf16[2048,2048]{1,0:T(8,128)(2,1)} %param.17), kind=kOutput, calls=%fused_computation.6 | convolution fusion | flops 1074003968 | bytes 9437184 | tf_op jit(solution)/shard_map/dot_general | solution.py:151
  (111 shorter events, 44.8 us)
Async XLA Ops:
  6.5 60.9 %all-gather.3.cloned.1.call-start = ((), (), s32[]{:S(2)}) async-start(), calls=%async_computation.6 | async-start | bytes 2621440 | tf_op jit(solution)/shard_map/all_gather | solution.py:74
  7.3 174.3 %all-gather.5.cloned.1.call-start = ((), (), s32[]{:S(2)}) async-start(), calls=%async_computation.7 | async-start | bytes 8519680 | tf_op jit(solution)/shard_map/all_gather | solution.py:79
  37.8 149.8 %all-to-all-start.2 = ((f32[64,2,512]{2,1,0:T(2,128)}), f32[64,2,512]{2,1,0:T(2,128)S(1)}, u32[]{:S(2)}, u32[]{:S(2)}) async-start(f32[64,2,512]{2,1,0:T(2,128)} %reshape.79), calls=%async_computation.2 | async-start | bytes 524288 | tf_op jit(solution)/shard_map/all_to_all | solution.py:102
  187.7 16.1 %all-to-all-start = ((f32[64,2,512]{2,1,0:T(2,128)}), f32[64,2,512]{2,1,0:T(2,128)S(1)}, u32[]{:S(2)}, u32[]{:S(2)}) async-start(f32[64,2,512]{2,1,0:T(2,128)} %reshape.78), calls=%async_computation | async-start | bytes 524288 | tf_op jit(solution)/shard_map/all_to_all | solution.py:95
  207.4 23.0 %all-to-all-start.3 = ((f32[2,128,2,512]{3,2,0,1:T(2,128)}), f32[2,128,2,512]{3,2,0,1:T(2,128)S(1)}, u32[]{:S(2)}, u32[]{:S(2)}) async-start(f32[2,128,2,512]{3,2,0,1:T(2,128)} %copy.40), calls=%async_computation.3 | async-start | bytes 2097152 | tf_op jit(solution)/shard_map/all_to_all | solution.py:118
  230.4 23.1 %all-to-all-start.1 = ((f32[2,128,2,512]{3,2,0,1:T(2,128)}), f32[2,128,2,512]{3,2,0,1:T(2,128)S(1)}, u32[]{:S(2)}, u32[]{:S(2)}) async-start(f32[2,128,2,512]{3,2,0,1:T(2,128)} %copy.34), calls=%async_computation.1 | async-start | bytes 2097152 | tf_op jit(solution)/shard_map/all_to_all | solution.py:111
  261.9 40.4 %copy-start = (bf16[128,512]{1,0:T(8,128)(2,1)S(1)}, bf16[128,512]{1,0:T(8,128)(2,1)}, u32[]{:S(2)}) copy-start(bf16[128,512]{1,0:T(8,128)(2,1)} %param.12) | copy-start | bytes 393220
  261.9 40.4 %copy-start.1 = (f32[512]{0:T(512)S(1)}, f32[512]{0:T(512)}, u32[]{:S(2)}) copy-start(f32[512]{0:T(512)} %param.16) | copy-start | bytes 6148
Sparse Core Ops, SparseCore 0:
  9.2 58.2 all-gather.2
  69.3 112.1 all-gather.4
where the time goes:
time: 334 us; the launch traced here: 331 us
  waiting for transfers between devices  173 us (52%)
  blocking collectives  53.1 us (16%)
  other arithmetic  28.6 us (9%)
  starting transfers between devices  25.9 us (8%)
  matrix products  25.2 us (8%)
  between operations  13.8 us (4%)
  local copies, waits for them, and re-layouts  10.7 us (3%)
    all_gather x1, waiting for transfers between devices, on_device(): lax.all_gather(value_weight, 'ctx', axis=0, tiled=True)  114 us
    all_to_all x1, blocking collectives, on_device(): lax.all_to_all(jnp.stack([back_real, back_imag]), 'ctx', split_axis=2, co...  22.4 us
    all_gather x1, waiting for transfers between devices, on_device(): whole = lax.all_gather(tokens, 'ch', axis=1, tiled=True)  19.3 us
    all_gather x1, blocking collectives, on_device(): lax.all_gather(mixed, 'ch', axis=1, tiled=True)  16.6 us
    all_to_all x1, waiting for transfers between devices, on_device(): lax.all_to_all(forward_columns(moved_kernel, cos_outer, sin_outer, twist_...  16.6 us
    add x16, other arithmetic, add_mode(): return (totals + term, None)  15.5 us
    all_to_all x1, blocking collectives, on_device(): lax.all_to_all(column_rows, 'ctx', split_axis=0, concat_axis=0, tiled=True)  14.1 us
    all_to_all x1, waiting for transfers between devices, on_device(): lax.all_to_all(forward_columns(moved_value, cos_outer, sin_outer, twist_c...  13.5 us
  transfers between devices with their start and end apart: 6, of which 5 were waited for; matrix products, arithmetic and copies ran while one was open for 13% of the time, Pallas kernels for 0%

commit v1 on v0

v1 whole, which is shorter than its diff:
```python
import jax
import jax.numpy as jnp
from jax import lax
from jax.experimental import pallas as pl
from jax.experimental.pallas import tpu as pltpu
from jax.sharding import PartitionSpec as P

MESH = pl.DeviceIdType.MESH
F32 = jnp.float32
BF16 = jnp.bfloat16

N = 4
ROWS = 128
FEAT = 2048
CH = 512
LANE = 128
BLOCK = 512
RUN = 32
RUNS = BLOCK // RUN
MODES = 16
SPAN = 8192.0
PIECES = 4
ORDER = (2, 1, 3, 0)


def cmul(ar, ai, br, bi):
    return ar * br - ai * bi, ar * bi + ai * br


def powers(rate, freq, t):
    mag = jnp.exp(-rate * t)
    angle = freq * t
    return mag * jnp.cos(angle), mag * jnp.sin(angle)


def make_tables(par, rate, pre, pim, filt, lev):
    rate[...] = par[0] * (1.0 / SPAN)
    amp = par[2] * jnp.sqrt(2.0 * rate[...])
    first = powers(rate[...], par[1], 1.0)
    lev[0], lev[1] = amp * first[0], amp * first[1]
    lev[2], lev[3] = powers(rate[...], par[1], float(RUN))
    lev[4], lev[5] = powers(rate[...], par[1], float(BLOCK))
    lev[6] = amp
    t = lax.broadcasted_iota(jnp.int32, (RUN, LANE), 0).astype(F32)

    def mode(m, total):
        re, im = powers(rate[pl.ds(m, 1), :], par[1, pl.ds(m, 1), :], t)
        pre[m], pim[m] = re, im
        return total + lev[6, pl.ds(m, 1), :] * re

    filt[...] = lax.fori_loop(0, MODES, mode, jnp.zeros((RUN, LANE), F32))


def run_states(value, runs, pre, pim, sre, sim):
    runs[0:RUN] = jnp.zeros((RUN, RUNS, LANE), F32)

    def split(t, _):
        runs[RUN + t] = value[pl.ds(t, RUNS, stride=RUN), :]
        return 0

    lax.fori_loop(0, RUN, split, 0)

    def modes(pair, _):
        zero = jnp.zeros((RUNS, LANE), F32)
        sums = [zero] * 4
        for t in range(RUN):
            v = runs[RUN + t]
            for i in range(2):
                m = pair * 2 + i
                sums[2 * i] += pre[m, RUN - 1 - t : RUN - t, :] * v
                sums[2 * i + 1] += pim[m, RUN - 1 - t : RUN - t, :] * v
        for i in range(2):
            rows = pl.ds(pl.multiple_of((pair * 2 + i) * RUNS, RUNS), RUNS)
            sre[rows, :] = sums[2 * i]
            sim[rows, :] = sums[2 * i + 1]
        return 0

    lax.fori_loop(0, MODES // 2, modes, 0)


def scan_runs(sre, sim, lev, carry, cre=None, cim=None):
    re, im = carry
    for b in range(RUNS):
        rows = pl.ds(b, MODES, stride=RUNS)
        if cre is not None:
            cre[rows, :], cim[rows, :] = cmul(re, im, lev[0], lev[1])
        re, im = cmul(re, im, lev[2], lev[3])
        re, im = re + sre[rows, :], im + sim[rows, :]
    return re, im


def carry_in(states, lev, block):
    re = im = jnp.zeros((MODES, LANE), F32)
    for other in range(N * N):
        new_re, new_im = cmul(re, im, lev[4], lev[5])
        new_re += states[other, 0:MODES, :].astype(F32)
        new_im += states[other, MODES : 2 * MODES, :].astype(F32)
        re = jnp.where(other < block, new_re, re)
        im = jnp.where(other < block, new_im, im)
    return re, im


def direct(runs, filt, near):
    group = 8
    for start in range(0, RUN, group):

        def lag(step, sums):
            gain = filt[pl.ds(step, 1), :]
            return tuple(
                total + gain * runs[RUN + start + i - step] for i, total in enumerate(sums)
            )

        sums = lax.fori_loop(
            0, start + group, lag, tuple(jnp.zeros((RUNS, LANE), F32) for _ in range(group))
        )
        for i in range(group):
            near[start + i] = sums[i]


def far_part(near, pre, pim, cre, cim, conv):
    group = 4

    def some(step, _):
        start = step * group
        sums = [near[start + i] for i in range(group)]
        for m in range(MODES):
            re = cre[m * RUNS : (m + 1) * RUNS, :]
            im = cim[m * RUNS : (m + 1) * RUNS, :]
            for i in range(group):
                row = pl.ds(start + i, 1)
                sums[i] += pre[m, row, :] * re - pim[m, row, :] * im
        for i in range(group):
            conv[pl.ds(start + i, RUNS, stride=RUN), :] = sums[i]
        return 0

    lax.fori_loop(0, RUN // group, some, 0)


def kernel(
    tokens, weight, gate, decay, freq, residue, skip, out_weight, out,
    tok, wf, gt, par, skip_v, ow, part_out, part_in, value, conv, runs, near, rate, pre, pim, filt, lev,
    sre, sim, cre, cim, states, mixed, seen, acc,
    loc, w1s, w1r, w2s, w2r, gs, gr, tzs, tzr, tcs, tcr, rss, rsr, sts, str_, mxs, mxr,
):
    ctx = lax.axis_index("ctx")
    h = lax.axis_index("ch")
    x, y, q = ctx // 16, (ctx // 4) % 4, ctx % 4
    block = ctx // 4
    across, beside = (q + 2) % 4, q + 1 - 2 * (q % 2)

    def remote(src, dst, ss, rs, where, ch):
        return pltpu.make_async_remote_copy(
            src_ref=src, dst_ref=dst, send_sem=ss, recv_sem=rs, device_id=(where, ch), device_id_type=MESH
        )

    def at(xx, yy, qq):
        return xx * 16 + yy * 4 + qq

    def quarter(i):
        return pl.ds(pl.multiple_of(i * LANE, LANE), LANE)

    sends = []

    def send(*args):
        copy = remote(*args)
        copy.start()
        sends.append(copy)

    def arrive(dst, ss, rs):
        remote(dst, dst, ss, rs, ctx, h).wait_recv()

    itself = (q == x) & (x == h)
    first = []
    for to in range(N):
        src, dst = weight.at[:, to * LANE : (to + 1) * LANE], wf.at[h, y, q]
        copy = remote(src, dst, w1s.at[to], w1r.at[h], at(q, y, to), x)
        mine = itself & (q == to)
        pl.when(jnp.logical_not(mine))(copy.start)
        pl.when(mine)(pltpu.make_async_copy(src, dst, w1r.at[h]).start)
        first.append((mine, copy))

    width = FEAT // PIECES
    for i in range(PIECES):
        cols = pl.ds(i * width, width)
        send(tokens.at[:, cols], tok.at[q, :, cols], tzs.at[i], tzr.at[i], at(x, y, across), h)
    send(tokens, tok.at[q], tcs.at[PIECES], tcr.at[PIECES], at(x, y, beside), h)
    for d in range(1, N):
        to = (q + d) % 4
        send(gate.at[:, quarter(to)], gt.at[q], gs.at[d - 1], gr.at[d - 1], at(x, y, to), h)

    local = [
        (decay.at[:, quarter(q)], par.at[0]),
        (freq.at[:, quarter(q)], par.at[1]),
        (residue.at[:, quarter(q)], par.at[2]),
        (skip.at[:, quarter(q)], skip_v),
        (tokens, tok.at[q]),
        (gate.at[:, quarter(q)], gt.at[q]),
        (out_weight, ow),
    ]
    local = [pltpu.make_async_copy(src, dst, loc.at[i]) for i, (src, dst) in enumerate(local)]
    for copy in local:
        copy.start()

    def ring(chunk, i, stage, d):
        back_x, back_y = (x + 4 - d) % 4, (y + 4 - d) % 4
        if (i + stage) % 2 == 0:
            to = at((x + d) % 4, y, q)
            if stage == 0:
                return wf.at[chunk, y, x], to, wf.at[chunk, y, back_x]
            return wf.at[chunk, :, x], to, wf.at[chunk, :, back_x]
        to = at(x, (y + d) % 4, q)
        if stage == 0:
            return wf.at[chunk, y, x], to, wf.at[chunk, back_y, x]
        return wf.at[chunk, y], to, wf.at[chunk, back_y]

    def spread(chunk, i, stage):
        for d in (2, 1, 3):
            src, to, _ = ring(chunk, i, stage, d)
            send(src, src, w2s.at[i, stage, d - 1], w2r.at[i, stage, d - 1], to, h)

    def spread_end(chunk, i, stage):
        for d in (1, 3, 2):
            _, _, dst = ring(chunk, i, stage, d)
            arrive(dst, w2s.at[i, stage, d - 1], w2r.at[i, stage, d - 1])

    chunks = [(h + d) % 4 for d in ORDER]
    for i, chunk in enumerate(chunks):
        arrive(wf.at[chunk, y, x], w1s.at[0], w1r.at[chunk])
        spread(chunk, i, 0)
    for i, chunk in enumerate(chunks):
        spread_end(chunk, i, 0)
        spread(chunk, i, 1)

    for copy in local[:3]:
        copy.wait()
    make_tables(par, rate, pre, pim, filt, lev)

    for i in range(PIECES):
        piece = tok.at[across, :, pl.ds(i * width, width)]
        arrive(piece, tzs.at[i], tzr.at[i])
        send(piece, piece, tcs.at[i], tcr.at[i], at(x, y, beside), h)
    arrive(tok.at[beside], tcs.at[PIECES], tcr.at[PIECES])
    for i in range(PIECES):
        piece = tok.at[(beside + 2) % 4, :, pl.ds(i * width, width)]
        arrive(piece, tcs.at[i], tcr.at[i])
    for copy in local[3:6]:
        copy.wait()

    for i, (d, chunk) in enumerate(zip(ORDER, chunks)):
        spread_end(chunk, i, 1)

        def rows(j, _):
            total = jnp.dot(
                tok[j], wf[chunk].reshape(FEAT, LANE), preferred_element_type=F32
            )
            here = pl.ds(pl.multiple_of(j * ROWS, ROWS), ROWS)
            if d == 0:
                value[here, :] = total
            else:
                part_out[d - 1, here, :] = total.astype(BF16)
            return 0

        lax.fori_loop(0, N, rows, 0)
        if d != 0:
            send(part_out.at[d - 1], part_in.at[d - 1], rss.at[d - 1], rsr.at[d - 1], ctx, chunk)
    for d in range(1, N):
        arrive(part_in.at[d - 1], rss.at[d - 1], rsr.at[d - 1])
        value[...] += part_in[d - 1].astype(F32)
    value[...] = value[...].astype(BF16).astype(F32)

    run_states(value, runs, pre, pim, sre, sim)
    zero = jnp.zeros((MODES, LANE), F32)
    end_re, end_im = scan_runs(sre, sim, lev, (zero, zero))
    states[block, 0:MODES, :] = end_re.astype(BF16)
    states[block, MODES : 2 * MODES, :] = end_im.astype(BF16)
    for d in range(1, N * N):
        to = (block + d) % 16
        send(states.at[block], states.at[block], sts.at[d - 1], str_.at[d - 1], to * 4 + q, h)
    direct(runs, filt, near)
    for d in range(1, N * N):
        arrive(states.at[(block + 16 - d) % 16], sts.at[d - 1], str_.at[d - 1])
    scan_runs(sre, sim, lev, carry_in(states, lev, block), cre, cim)
    far_part(near, pre, pim, cre, cim, conv)

    for d in range(1, N):
        arrive(gt.at[(q + 4 - d) % 4], gs.at[d - 1], gr.at[d - 1])
    for j in range(N):
        here = pl.ds(j * ROWS, ROWS)
        total = conv[here, :] + skip_v[...] * value[here, :]
        mixed[here, :] = (gt[j].astype(F32) * total).astype(BF16)

    own = None
    for dh in (2, 1, 3, 0):
        for dq in range(N):
            to = (q + dq) % 4
            src = mixed.at[pl.ds(pl.multiple_of(to * ROWS, ROWS), ROWS), :]
            dst = seen.at[h, :, quarter(q)]
            sem = mxs.at[dh * N + dq], mxr.at[dh * N + dq]
            if dh == 0 and dq == 0:
                own = pltpu.make_async_copy(src, dst, sem[1])
                own.start()
            else:
                send(src, dst, *sem, at(x, y, to), (h + dh) % 4)
    local[6].wait()
    for step, dh in enumerate((0, 1, 3, 2)):
        source = (h + 4 - dh) % 4
        for dq in range(N):
            dst = seen.at[source, :, quarter((q + 4 - dq) % 4)]
            if dh == 0 and dq == 0:
                own.wait()
            else:
                arrive(dst, mxs.at[dh * N + dq], mxr.at[dh * N + dq])

        def columns(n, _):
            cols = pl.ds(pl.multiple_of(n * 512, 512), 512)
            deep = pl.ds(pl.multiple_of(source * CH, CH), CH)
            total = jnp.dot(seen[source], ow[deep, cols], preferred_element_type=F32)
            if step > 0:
                total += acc[:, cols]
            if step < N - 1:
                acc[:, cols] = total
            else:
                out[:, cols] = total.astype(BF16)
            return 0

        lax.fori_loop(0, FEAT // 512, columns, 0)

    for copy in sends:
        copy.wait_send()
    for mine, copy in first:
        pl.when(jnp.logical_not(mine))(copy.wait_send)


def on_device(tokens, weight, gate, decay, freq, residue, skip, out_weight):
    vmem, dma = pltpu.VMEM, pltpu.SemaphoreType.DMA
    return pl.pallas_call(
        kernel,
        out_shape=jax.ShapeDtypeStruct((ROWS, FEAT), BF16),
        in_specs=[pl.BlockSpec(memory_space=pl.ANY)] * 8,
        out_specs=pl.BlockSpec(memory_space=pltpu.VMEM),
        scratch_shapes=[
            vmem((N, ROWS, FEAT), BF16),
            vmem((N, N, N, ROWS, LANE), BF16),
            vmem((N, ROWS, LANE), BF16),
            vmem((3, MODES, LANE), F32),
            vmem((1, LANE), F32),
            vmem((N * CH, FEAT), BF16),
            vmem((N - 1, BLOCK, LANE), BF16),
            vmem((N - 1, BLOCK, LANE), BF16),
            vmem((BLOCK, LANE), F32),
            vmem((BLOCK, LANE), F32),
            vmem((2 * RUN, RUNS, LANE), F32),
            vmem((RUN, RUNS, LANE), F32),
            vmem((MODES, LANE), F32),
            vmem((MODES, RUN, LANE), F32),
            vmem((MODES, RUN, LANE), F32),
            vmem((RUN, LANE), F32),
            vmem((7, MODES, LANE), F32),
            vmem((MODES * RUNS, LANE), F32),
            vmem((MODES * RUNS, LANE), F32),
            vmem((MODES * RUNS, LANE), F32),
            vmem((MODES * RUNS, LANE), F32),
            vmem((N * N, 2 * MODES, LANE), BF16),
            vmem((BLOCK, LANE), BF16),
            vmem((N, ROWS, CH), BF16),
            vmem((ROWS, FEAT), F32),
            dma((7,)),
            dma((N,)), dma((N,)),
            dma((N, 2, 3)), dma((N, 2, 3)),
            dma((3,)), dma((3,)),
            dma((PIECES,)), dma((PIECES,)),
            dma((PIECES + 1,)), dma((PIECES + 1,)),
            dma((3,)), dma((3,)),
            dma((15,)), dma((15,)),
            dma((16,)), dma((16,)),
        ],
        compiler_params=pltpu.CompilerParams(
            has_side_effects=True, vmem_limit_bytes=48 * 1024 * 1024
        ),
    )(tokens, weight, gate, decay, freq, residue, skip.reshape(1, CH), out_weight)


def solution(mesh):
    placed = (
        P("ctx", "ch"),
        P("ctx", "ch"),
        P("ctx", "ch"),
        P(None, "ch"),
        P(None, "ch"),
        P(None, "ch"),
        P("ch"),
        P(None, "ch"),
    )
    return jax.shard_map(
        on_device, mesh=mesh, in_specs=placed, out_specs=P("ctx", "ch"), check_vma=False
    )
```

time: 334 us -> 86.1 us (0.26)
  waiting for transfers between devices: 173 us -> 0 us
  Pallas kernels: 0 us -> 79.1 us
  blocking collectives: 53.1 us -> 0 us
  other arithmetic: 28.6 us -> 0 us
  starting transfers between devices: 25.9 us -> 0 us
  matrix products: 25.2 us -> 0 us
  between operations: 13.8 us -> 0.02 us
  local copies, waits for them, and re-layouts: 10.7 us -> 6.6 us
    all_gather x2 -> x0, waiting for transfers between devices: 133 us -> none  [the longest x1 114 us: on_device(): lax.all_gather(value_weight, 'ctx', axis=0, tiled=True)]
    pallas_call x0 -> x1, Pallas kernels: none -> 79.1 us  [on_device(): pl.pallas_call(kernel, out_shape=jax.ShapeDtypeStruct((ROWS, FEAT), BF16)...]
    all_to_all x4 -> x0, waiting for transfers between devices: 38.5 us -> none  [the longest x1 16.6 us: on_device(): lax.all_to_all(forward_columns(moved_kernel, cos_outer, sin_outer, twist_...]
    all_to_all x2 -> x0, blocking collectives: 36.5 us -> none  [the longest x1 22.4 us: on_device(): lax.all_to_all(jnp.stack([back_real, back_imag]), 'ctx', split_axis=2, co...]
    all_to_all x4 -> x0, starting transfers between devices: 25.9 us -> none  [the longest x1 10.3 us: on_device(): lax.all_to_all(kernel.reshape(shards, group_rows, channels), 'ctx', split...]
    dot_general x20 -> x0, matrix products: 25.2 us -> none  [the longest x1 5.46 us: on_device(): jnp.dot(lax.all_gather(mixed, 'ch', axis=1, tiled=True), out_weight, pref...]
    all_gather x1 -> x0, blocking collectives: 16.6 us -> none  [on_device(): lax.all_gather(mixed, 'ch', axis=1, tiled=True)]
    add x17 -> x0, other arithmetic: 15.5 us -> none  [the longest x16 15.5 us: add_mode(): return (totals + term, None)]
  transfers between devices with their start and end apart: 6 -> 0, of which waited for: 5 -> 0; matrix products, arithmetic and copies ran while one was open for 13% -> 0% of each run, Pallas kernels for 0% -> 0%
where the time goes in v1:
time: 86.1 us; the launch traced here: 85.7 us
  Pallas kernels  79.1 us (92%)
  local copies, waits for them, and re-layouts  6.6 us (8%)
    pallas_call x1, Pallas kernels, on_device(): pl.pallas_call(kernel, out_shape=jax.ShapeDtypeStruct((ROWS, FEAT), BF16)...  79.1 us
    unnamed x15, local copies, waits for them, and re-layouts  6.6 us

profile of v1, /device:TPU:1, one launch (start us, length us, event | category | flops | bytes accessed | tf_op | source)
XLA Modules:
  0.0 85.7 jit_solution(3180182804928258066)
XLA Ops:
  0.0 0.0 copy-start
  0.0 1.0 %copy-done = bf16[128,2048]{1,0:T(8,128)(2,1)S(1)} copy-done((bf16[128,2048]{1,0:T(8,128)(2,1)S(1)}, bf16[128,2048]{1,0:T(8,128)(2,1)}, u32[]{:S(2)}) %copy-start) | copy-done | bytes 524312
  1.0 0.0 copy-start.1
  1.0 0.9 %copy-done.1 = bf16[128,512]{1,0:T(8,128)(2,1)S(1)} copy-done((bf16[128,512]{1,0:T(8,128)(2,1)S(1)}, bf16[128,512]{1,0:T(8,128)(2,1)}, u32[]{:S(2)}) %copy-start.1) | copy-done | bytes 131096
  1.9 0.0 copy-start.2
  1.9 0.9 %copy-done.2 = bf16[128,512]{1,0:T(8,128)(2,1)S(1)} copy-done((bf16[128,512]{1,0:T(8,128)(2,1)S(1)}, bf16[128,512]{1,0:T(8,128)(2,1)}, u32[]{:S(2)}) %copy-start.2) | copy-done | bytes 131096
  2.9 0.0 copy-start.3
  2.9 0.8 copy-done.3
  3.6 0.0 copy-start.4
  3.6 0.8 copy-done.4
  4.4 0.0 copy-start.5
  4.4 0.8 copy-done.5
  5.1 0.0 copy-start.6
  5.1 0.7 copy-done.6
  5.8 79.1 %shard_map.82 = bf16[128,2048]{1,0:T(8,128)(2,1)S(1)} custom-call(bf16[128,2048]{1,0:T(8,128)(2,1)S(1)} %copy-done, bf16[128,512]{1,0:T(8,128)(2,1)S(1)} %copy-done.1, bf16[128,512]{1,0:T(8,128)(2,1)S(1)} %copy-done.2, f32[16,512]{1,0:T(8,128)S(1)} %copy-done.3, f32[16,512]{1,0:T(8,128)S(1)} %copy-done.4, f32[16,512]{1,0:T(8,128)S(1)} %copy-done.5, ...), custom_call_target="tpu_custom_call" | custom-call | tf_op jit(solution)/shard_map/pallas_call | solution.py:336
  84.9 0.8 copy.10
Async XLA Ops:
  0.0 1.0 %copy-start = (bf16[128,2048]{1,0:T(8,128)(2,1)S(1)}, bf16[128,2048]{1,0:T(8,128)(2,1)}, u32[]{:S(2)}) copy-start(bf16[128,2048]{1,0:T(8,128)(2,1)} %tokens.1) | copy-start | bytes 1572868
  1.0 0.9 %copy-start.1 = (bf16[128,512]{1,0:T(8,128)(2,1)S(1)}, bf16[128,512]{1,0:T(8,128)(2,1)}, u32[]{:S(2)}) copy-start(bf16[128,512]{1,0:T(8,128)(2,1)} %weight.1) | copy-start | bytes 393220
  1.9 0.9 %copy-start.2 = (bf16[128,512]{1,0:T(8,128)(2,1)S(1)}, bf16[128,512]{1,0:T(8,128)(2,1)}, u32[]{:S(2)}) copy-start(bf16[128,512]{1,0:T(8,128)(2,1)} %gate.1) | copy-start | bytes 393220
  2.9 0.8 copy-start.3
  3.6 0.8 copy-start.4
  4.4 0.8 copy-start.5
  5.1 0.7 copy-start.6

commit v2 on v1

--- a/solution.py
+++ b/solution.py
@@ -13,6 +13,7 @@
 ROWS = 128
 FEAT = 2048
 CH = 512
+BAND = ROWS // N
 LANE = 128
 BLOCK = 512
 RUN = 32
@@ -20,6 +21,7 @@
 MODES = 16
 SPAN = 8192.0
 PIECES = 4
+SEMS = 112
 ORDER = (2, 1, 3, 0)
 
 
@@ -139,8 +141,7 @@
 def kernel(
     tokens, weight, gate, decay, freq, residue, skip, out_weight, out,
     tok, wf, gt, par, skip_v, ow, part_out, part_in, value, conv, runs, near, rate, pre, pim, filt, lev,
-    sre, sim, cre, cim, states, mixed, seen, acc,
-    loc, w1s, w1r, w2s, w2r, gs, gr, tzs, tzr, tcs, tcr, rss, rsr, sts, str_, mxs, mxr,
+    sre, sim, cre, cim, states, mixed, seen, acc, lifted, loc, sent_sem, got_sem,
 ):
     ctx = lax.axis_index("ctx")
     h = lax.axis_index("ch")
@@ -148,45 +149,56 @@
     block = ctx // 4
     across, beside = (q + 2) % 4, q + 1 - 2 * (q % 2)
 
-    def remote(src, dst, ss, rs, where, ch):
-        return pltpu.make_async_remote_copy(
-            src_ref=src, dst_ref=dst, send_sem=ss, recv_sem=rs, device_id=(where, ch), device_id_type=MESH
-        )
-
     def at(xx, yy, qq):
         return xx * 16 + yy * 4 + qq
 
     def quarter(i):
         return pl.ds(pl.multiple_of(i * LANE, LANE), LANE)
 
+    def band(i):
+        return pl.ds(pl.multiple_of(i * BAND, BAND), BAND)
+
+    names = {}
     sends = []
 
-    def send(*args):
-        copy = remote(*args)
+    def sem(name):
+        return names.setdefault(name, len(names))
+
+    def remote(src, dst, out_id, in_id, where, ch):
+        return pltpu.make_async_remote_copy(
+            src_ref=src, dst_ref=dst, send_sem=sent_sem.at[out_id], recv_sem=got_sem.at[in_id],
+            device_id=(where, ch), device_id_type=MESH,
+        )
+
+    def send(name, src, dst, where, ch):
+        i = sem(name)
+        copy = remote(src, dst, i, i, where, ch)
         copy.start()
         sends.append(copy)
 
-    def arrive(dst, ss, rs):
-        remote(dst, dst, ss, rs, ctx, h).wait_recv()
-
-    itself = (q == x) & (x == h)
-    first = []
-    for to in range(N):
-        src, dst = weight.at[:, to * LANE : (to + 1) * LANE], wf.at[h, y, q]
-        copy = remote(src, dst, w1s.at[to], w1r.at[h], at(q, y, to), x)
-        mine = itself & (q == to)
-        pl.when(jnp.logical_not(mine))(copy.start)
-        pl.when(mine)(pltpu.make_async_copy(src, dst, w1r.at[h]).start)
-        first.append((mine, copy))
-
-    width = FEAT // PIECES
-    for i in range(PIECES):
-        cols = pl.ds(i * width, width)
-        send(tokens.at[:, cols], tok.at[q, :, cols], tzs.at[i], tzr.at[i], at(x, y, across), h)
-    send(tokens, tok.at[q], tcs.at[PIECES], tcr.at[PIECES], at(x, y, beside), h)
+    def arrive(name, dst):
+        i = sem(name)
+        remote(dst, dst, i, i, ctx, h).wait_recv()
+
+    barrier = pltpu.get_barrier_semaphore()
+
+    def greet(where, ch):
+        pl.semaphore_signal(barrier, inc=1, device_id=(where, ch), device_id_type=MESH)
+
+    for d in range(1, N * N):
+        greet((block + d) % 16 * 4 + q, h)
+        greet(at(x, y, (q + d) % 4), (h + d // 4) % 4)
+    pl.semaphore_wait(barrier, 2 * (N * N - 1))
+
+    for d in (2, 1, 3):
+        to = (x + d) % 4
+        send(("lift", d), weight.at[band(to), :], lifted.at[x], at(to, y, q), h)
+    keep = pltpu.make_async_copy(weight.at[band(x), :], lifted.at[x], loc.at[8])
+    keep.start()
+
     for d in range(1, N):
         to = (q + d) % 4
-        send(gate.at[:, quarter(to)], gt.at[q], gs.at[d - 1], gr.at[d - 1], at(x, y, to), h)
+        send(("gate", d), gate.at[:, quarter(to)], gt.at[q], at(x, y, to), h)
 
     local = [
         (decay.at[:, quarter(q)], par.at[0]),
@@ -201,31 +213,58 @@
     for copy in local:
         copy.start()
 
+    keep.wait()
+    for d in (1, 3, 2):
+        arrive(("lift", d), lifted.at[(x + 4 - d) % 4])
+    keep = []
+    for dh in (2, 1, 3, 0):
+        for dq in range(N):
+            to, ch = (q + dq) % 4, (h + dh) % 4
+            src, dst = lifted.at[ch, :, quarter(to)], wf.at[h, y, q, band(x), :]
+            if dh == 0 and dq == 0:
+                keep.append(pltpu.make_async_copy(src, dst, loc.at[8]))
+                keep[0].start()
+            else:
+                send(("weight", dh, dq), src, dst, at(x, y, to), ch)
+
+    width = FEAT // PIECES
+    for i in range(PIECES):
+        cols = pl.ds(i * width, width)
+        send(("across", i), tokens.at[:, cols], tok.at[q, :, cols], at(x, y, across), h)
+    send("beside", tokens, tok.at[q], at(x, y, beside), h)
+
+    def weight_end(d):
+        dh = (4 - d) % 4
+        for dq in range(N):
+            if dh == 0 and dq == 0:
+                keep[0].wait()
+            else:
+                arrive(("weight", dh, dq), wf.at[(h + d) % 4, y, (q + 4 - dq) % 4, band(x), :])
+
     def ring(chunk, i, stage, d):
         back_x, back_y = (x + 4 - d) % 4, (y + 4 - d) % 4
-        if (i + stage) % 2 == 0:
-            to = at((x + d) % 4, y, q)
-            if stage == 0:
-                return wf.at[chunk, y, x], to, wf.at[chunk, y, back_x]
-            return wf.at[chunk, :, x], to, wf.at[chunk, :, back_x]
-        to = at(x, (y + d) % 4, q)
+        along_x, along_y = at((x + d) % 4, y, q), at(x, (y + d) % 4, q)
         if stage == 0:
-            return wf.at[chunk, y, x], to, wf.at[chunk, back_y, x]
-        return wf.at[chunk, y], to, wf.at[chunk, back_y]
+            src = wf.at[chunk, y, :, band(x), :]
+            if i % 2 == 0:
+                return src, along_x, wf.at[chunk, y, :, band(back_x), :]
+            return src, along_y, wf.at[chunk, back_y, :, band(x), :]
+        if i % 2 == 0:
+            return wf.at[chunk, y], along_y, wf.at[chunk, back_y]
+        return wf.at[chunk, :, :, band(x), :], along_x, wf.at[chunk, :, :, band(back_x), :]
 
     def spread(chunk, i, stage):
         for d in (2, 1, 3):
             src, to, _ = ring(chunk, i, stage, d)
-            send(src, src, w2s.at[i, stage, d - 1], w2r.at[i, stage, d - 1], to, h)
+            send(("spread", i, stage, d), src, src, to, h)
 
     def spread_end(chunk, i, stage):
         for d in (1, 3, 2):
-            _, _, dst = ring(chunk, i, stage, d)
-            arrive(dst, w2s.at[i, stage, d - 1], w2r.at[i, stage, d - 1])
+            arrive(("spread", i, stage, d), ring(chunk, i, stage, d)[2])
 
     chunks = [(h + d) % 4 for d in ORDER]
-    for i, chunk in enumerate(chunks):
-        arrive(wf.at[chunk, y, x], w1s.at[0], w1r.at[chunk])
+    for i, (d, chunk) in enumerate(zip(ORDER, chunks)):
+        weight_end(d)
         spread(chunk, i, 0)
     for i, chunk in enumerate(chunks):
         spread_end(chunk, i, 0)
@@ -237,12 +276,11 @@
 
     for i in range(PIECES):
         piece = tok.at[across, :, pl.ds(i * width, width)]
-        arrive(piece, tzs.at[i], tzr.at[i])
-        send(piece, piece, tcs.at[i], tcr.at[i], at(x, y, beside), h)
-    arrive(tok.at[beside], tcs.at[PIECES], tcr.at[PIECES])
+        arrive(("across", i), piece)
+        send(("along", i), piece, piece, at(x, y, beside), h)
+    arrive("beside", tok.at[beside])
     for i in range(PIECES):
-        piece = tok.at[(beside + 2) % 4, :, pl.ds(i * width, width)]
-        arrive(piece, tcs.at[i], tcr.at[i])
+        arrive(("along", i), tok.at[(beside + 2) % 4, :, pl.ds(i * width, width)])
     for copy in local[3:6]:
         copy.wait()
 
@@ -262,9 +300,9 @@
 
         lax.fori_loop(0, N, rows, 0)
         if d != 0:
-            send(part_out.at[d - 1], part_in.at[d - 1], rss.at[d - 1], rsr.at[d - 1], ctx, chunk)
+            send(("sum", d), part_out.at[d - 1], part_in.at[d - 1], ctx, chunk)
     for d in range(1, N):
-        arrive(part_in.at[d - 1], rss.at[d - 1], rsr.at[d - 1])
+        arrive(("sum", d), part_in.at[d - 1])
         value[...] += part_in[d - 1].astype(F32)
     value[...] = value[...].astype(BF16).astype(F32)
 
@@ -275,15 +313,15 @@
     states[block, MODES : 2 * MODES, :] = end_im.astype(BF16)
     for d in range(1, N * N):
         to = (block + d) % 16
-        send(states.at[block], states.at[block], sts.at[d - 1], str_.at[d - 1], to * 4 + q, h)
+        send(("state", d), states.at[block], states.at[block], to * 4 + q, h)
     direct(runs, filt, near)
     for d in range(1, N * N):
-        arrive(states.at[(block + 16 - d) % 16], sts.at[d - 1], str_.at[d - 1])
+        arrive(("state", d), states.at[(block + 16 - d) % 16])
     scan_runs(sre, sim, lev, carry_in(states, lev, block), cre, cim)
     far_part(near, pre, pim, cre, cim, conv)
 
     for d in range(1, N):
-        arrive(gt.at[(q + 4 - d) % 4], gs.at[d - 1], gr.at[d - 1])
+        arrive(("gate", d), gt.at[(q + 4 - d) % 4])
     for j in range(N):
         here = pl.ds(j * ROWS, ROWS)
         total = conv[here, :] + skip_v[...] * value[here, :]
@@ -295,21 +333,19 @@
             to = (q + dq) % 4
             src = mixed.at[pl.ds(pl.multiple_of(to * ROWS, ROWS), ROWS), :]
             dst = seen.at[h, :, quarter(q)]
-            sem = mxs.at[dh * N + dq], mxr.at[dh * N + dq]
             if dh == 0 and dq == 0:
-                own = pltpu.make_async_copy(src, dst, sem[1])
+                own = pltpu.make_async_copy(src, dst, loc.at[7])
                 own.start()
             else:
-                send(src, dst, *sem, at(x, y, to), (h + dh) % 4)
+                send(("mixed", dh, dq), src, dst, at(x, y, to), (h + dh) % 4)
     local[6].wait()
     for step, dh in enumerate((0, 1, 3, 2)):
         source = (h + 4 - dh) % 4
         for dq in range(N):
-            dst = seen.at[source, :, quarter((q + 4 - dq) % 4)]
             if dh == 0 and dq == 0:
                 own.wait()
             else:
-                arrive(dst, mxs.at[dh * N + dq], mxr.at[dh * N + dq])
+                arrive(("mixed", dh, dq), seen.at[source, :, quarter((q + 4 - dq) % 4)])
 
         def columns(n, _):
             cols = pl.ds(pl.multiple_of(n * 512, 512), 512)
@@ -327,8 +363,7 @@
 
     for copy in sends:
         copy.wait_send()
-    for mine, copy in first:
-        pl.when(jnp.logical_not(mine))(copy.wait_send)
+    assert len(names) <= SEMS
 
 
 def on_device(tokens, weight, gate, decay, freq, residue, skip, out_weight):
@@ -364,18 +399,12 @@
             vmem((BLOCK, LANE), BF16),
             vmem((N, ROWS, CH), BF16),
             vmem((ROWS, FEAT), F32),
-            dma((7,)),
-            dma((N,)), dma((N,)),
-            dma((N, 2, 3)), dma((N, 2, 3)),
-            dma((3,)), dma((3,)),
-            dma((PIECES,)), dma((PIECES,)),
-            dma((PIECES + 1,)), dma((PIECES + 1,)),
-            dma((3,)), dma((3,)),
-            dma((15,)), dma((15,)),
-            dma((16,)), dma((16,)),
+            vmem((N, BAND, CH), BF16),
+            dma((9,)),
+            dma((SEMS,)), dma((SEMS,)),
         ],
         compiler_params=pltpu.CompilerParams(
-            has_side_effects=True, vmem_limit_bytes=48 * 1024 * 1024
+            collective_id=0, has_side_effects=True, vmem_limit_bytes=60 * 1024 * 1024
         ),
     )(tokens, weight, gate, decay, freq, residue, skip.reshape(1, CH), out_weight)
 

time: 86.1 us -> 76.5 us (0.89)
  local copies, waits for them, and re-layouts: 6.6 us -> 1.88 us
  Pallas kernels: 79.1 us -> 74.5 us
    unnamed x15 -> x1, local copies, waits for them, and re-layouts: 6.6 us -> 1.88 us
    pallas_call x1, Pallas kernels: 79.1 us -> 74.5 us  [on_device(): pl.pallas_call(kernel, out_shape=jax.ShapeDtypeStruct((ROWS, FEAT), BF16)...]
where the time goes in v2:
time: 76.5 us; the launch traced here: 76.4 us
  Pallas kernels  74.5 us (97%)
  local copies, waits for them, and re-layouts  1.88 us (2%)
    pallas_call x1, Pallas kernels, on_device(): pl.pallas_call(kernel, out_shape=jax.ShapeDtypeStruct((ROWS, FEAT), BF16)...  74.5 us
    unnamed x1, local copies, waits for them, and re-layouts  1.88 us

profile of v2, /device:TPU:1, one launch (start us, length us, event | category | flops | bytes accessed | tf_op | source)
XLA Modules:
  0.0 76.4 jit_solution(4792341449618215351)
XLA Ops:
  0.0 74.5 %shard_map.82 = bf16[128,2048]{1,0:T(8,128)(2,1)} custom-call(bf16[128,2048]{1,0:T(8,128)(2,1)} %tokens.1, bf16[128,512]{1,0:T(8,128)(2,1)} %weight.1, bf16[128,512]{1,0:T(8,128)(2,1)} %gate.1, f32[16,512]{1,0:T(8,128)} %decay.1, f32[16,512]{1,0:T(8,128)} %freq.1, f32[16,512]{1,0:T(8,128)} %residue.1, f32[1,512]{1,0:T(1,128)} %bitcast.1, ...), custom_call_target="tpu_custom_call" | custom-call | tf_op jit(solution)/shard_map/pallas_call | solution.py:371
  74.5 1.9 %copy.10 = bf16[128,2048]{1,0:T(8,128)(2,1)} copy(bf16[128,2048]{1,0:T(8,128)(2,1)} %shard_map.82) | data formatting | bytes 1048576

commit v3 on v2

--- a/solution.py
+++ b/solution.py
@@ -21,7 +21,7 @@
 MODES = 16
 SPAN = 8192.0
 PIECES = 4
-SEMS = 112
+SEMS = 160
 ORDER = (2, 1, 3, 0)
 
 
@@ -140,7 +140,7 @@
 
 def kernel(
     tokens, weight, gate, decay, freq, residue, skip, out_weight, out,
-    tok, wf, gt, par, skip_v, ow, part_out, part_in, value, conv, runs, near, rate, pre, pim, filt, lev,
+    tok, wf, gt, par, skip_v, ow, part_out, part_in, passed, value, conv, runs, near, rate, pre, pim, filt, lev,
     sre, sim, cre, cim, states, mixed, seen, acc, lifted, loc, sent_sem, got_sem,
 ):
     ctx = lax.axis_index("ctx")
@@ -159,7 +159,8 @@
         return pl.ds(pl.multiple_of(i * BAND, BAND), BAND)
 
     names = {}
-    sends = []
+    seen_names = set()
+    sends = {}
 
     def sem(name):
         return names.setdefault(name, len(names))
@@ -174,11 +175,16 @@
         i = sem(name)
         copy = remote(src, dst, i, i, where, ch)
         copy.start()
-        sends.append(copy)
+        sends[name] = copy
+
+    def sent(name):
+        sends.pop(name).wait_send()
 
     def arrive(name, dst):
-        i = sem(name)
-        remote(dst, dst, i, i, ctx, h).wait_recv()
+        if name not in seen_names:
+            seen_names.add(name)
+            i = sem(name)
+            remote(dst, dst, i, i, ctx, h).wait_recv()
 
     barrier = pltpu.get_barrier_semaphore()
 
@@ -195,10 +201,6 @@
         send(("lift", d), weight.at[band(to), :], lifted.at[x], at(to, y, q), h)
     keep = pltpu.make_async_copy(weight.at[band(x), :], lifted.at[x], loc.at[8])
     keep.start()
-
-    for d in range(1, N):
-        to = (q + d) % 4
-        send(("gate", d), gate.at[:, quarter(to)], gt.at[q], at(x, y, to), h)
 
     local = [
         (decay.at[:, quarter(q)], par.at[0]),
@@ -213,19 +215,28 @@
     for copy in local:
         copy.start()
 
-    keep.wait()
-    for d in (1, 3, 2):
-        arrive(("lift", d), lifted.at[(x + 4 - d) % 4])
-    keep = []
-    for dh in (2, 1, 3, 0):
+    base = [sem(("weight", i)) for i in range(N * N)][0]
+    last = [sem(("weight sent", i)) for i in range(N * N)][0]
+    onward = []
+    for d in (0, 1, 3, 2):
+        ch = (x + 4 - d) % 4
+        if d == 0:
+            keep.wait()
+        else:
+            arrive(("lift", d), lifted.at[ch])
         for dq in range(N):
-            to, ch = (q + dq) % 4, (h + dh) % 4
+            to = (q + dq) % 4
             src, dst = lifted.at[ch, :, quarter(to)], wf.at[h, y, q, band(x), :]
-            if dh == 0 and dq == 0:
-                keep.append(pltpu.make_async_copy(src, dst, loc.at[8]))
-                keep[0].start()
+            got = base + (ch + 4 - h) % 4 * N + dq
+            copy = remote(src, dst, last + d * N + dq, got, at(x, y, to), ch)
+            if dq == 0:
+                away = ch != h
+                pl.when(away)(copy.start)
+                pl.when(ch == h)(pltpu.make_async_copy(src, dst, got_sem.at[got]).start)
+                onward.append((away, copy))
             else:
-                send(("weight", dh, dq), src, dst, at(x, y, to), ch)
+                copy.start()
+                sends["weight", d, dq] = copy
 
     width = FEAT // PIECES
     for i in range(PIECES):
@@ -234,76 +245,111 @@
     send("beside", tokens, tok.at[q], at(x, y, beside), h)
 
     def weight_end(d):
-        dh = (4 - d) % 4
         for dq in range(N):
-            if dh == 0 and dq == 0:
-                keep[0].wait()
-            else:
-                arrive(("weight", dh, dq), wf.at[(h + d) % 4, y, (q + 4 - dq) % 4, band(x), :])
-
-    def ring(chunk, i, stage, d):
+            i = base + (4 - d) % 4 * N + dq
+            dst = wf.at[(h + d) % 4, y, (q + 4 - dq) % 4, band(x), :]
+            remote(dst, dst, i, i, ctx, h).wait_recv()
+
+    def ring(chunk, g, stage, d):
         back_x, back_y = (x + 4 - d) % 4, (y + 4 - d) % 4
         along_x, along_y = at((x + d) % 4, y, q), at(x, (y + d) % 4, q)
+        some = pl.ds(2 * g, 2)
         if stage == 0:
-            src = wf.at[chunk, y, :, band(x), :]
-            if i % 2 == 0:
-                return src, along_x, wf.at[chunk, y, :, band(back_x), :]
-            return src, along_y, wf.at[chunk, back_y, :, band(x), :]
-        if i % 2 == 0:
-            return wf.at[chunk, y], along_y, wf.at[chunk, back_y]
-        return wf.at[chunk, :, :, band(x), :], along_x, wf.at[chunk, :, :, band(back_x), :]
-
-    def spread(chunk, i, stage):
-        for d in (2, 1, 3):
-            src, to, _ = ring(chunk, i, stage, d)
-            send(("spread", i, stage, d), src, src, to, h)
-
-    def spread_end(chunk, i, stage):
-        for d in (1, 3, 2):
-            arrive(("spread", i, stage, d), ring(chunk, i, stage, d)[2])
+            src = wf.at[chunk, y, some, band(x), :]
+            if g == 0:
+                return src, along_x, wf.at[chunk, y, some, band(back_x), :]
+            return src, along_y, wf.at[chunk, back_y, some, band(x), :]
+        if g == 0:
+            return wf.at[chunk, y, some], along_y, wf.at[chunk, back_y, some]
+        return wf.at[chunk, :, some, band(x), :], along_x, wf.at[chunk, :, some, band(back_x), :]
 
     chunks = [(h + d) % 4 for d in ORDER]
-    for i, (d, chunk) in enumerate(zip(ORDER, chunks)):
+    ways = [(g, d) for d in (2, 1, 3) for g in range(2)]
+
+    def spread(i, stage):
+        for g, d in ways:
+            src, to, _ = ring(chunks[i], g, stage, d)
+            send(("spread", i, g, stage, d), src, src, to, h)
+
+    def spread_end(i, stage):
+        for g, d in ways:
+            arrive(("spread", i, g, stage, d), ring(chunks[i], g, stage, d)[2])
+
+    def spread_sent(i):
+        for g, d in ways:
+            sent(("spread", i, g, 1, d))
+
+    def forward(i):
+        piece = tok.at[across, :, pl.ds(i * width, width)]
+        arrive(("across", i), piece)
+        send(("along", i), piece, piece, at(x, y, beside), h)
+
+    for d in (0, 1, 3, 2):
         weight_end(d)
-        spread(chunk, i, 0)
-    for i, chunk in enumerate(chunks):
-        spread_end(chunk, i, 0)
-        spread(chunk, i, 1)
-
+        spread(ORDER.index(d), 0)
+    for i in (0, 1):
+        spread_end(i, 0)
+        spread(i, 1)
     for copy in local[:3]:
         copy.wait()
     make_tables(par, rate, pre, pim, filt, lev)
-
-    for i in range(PIECES):
-        piece = tok.at[across, :, pl.ds(i * width, width)]
-        arrive(("across", i), piece)
-        send(("along", i), piece, piece, at(x, y, beside), h)
+    forward(0)
+    forward(1)
+    spread_sent(0)
+    spread_end(2, 0)
+    spread(2, 1)
+    forward(2)
+    spread_sent(1)
+    spread_end(3, 0)
+    spread(3, 1)
+    forward(3)
     arrive("beside", tok.at[beside])
     for i in range(PIECES):
         arrive(("along", i), tok.at[(beside + 2) % 4, :, pl.ds(i * width, width)])
     for copy in local[3:6]:
         copy.wait()
 
-    for i, (d, chunk) in enumerate(zip(ORDER, chunks)):
-        spread_end(chunk, i, 1)
-
-        def rows(j, _):
-            total = jnp.dot(
-                tok[j], wf[chunk].reshape(FEAT, LANE), preferred_element_type=F32
-            )
-            here = pl.ds(pl.multiple_of(j * ROWS, ROWS), ROWS)
-            if d == 0:
-                value[here, :] = total
-            else:
-                part_out[d - 1, here, :] = total.astype(BF16)
-            return 0
-
-        lax.fori_loop(0, N, rows, 0)
-        if d != 0:
-            send(("sum", d), part_out.at[d - 1], part_in.at[d - 1], ctx, chunk)
     for d in range(1, N):
-        arrive(("sum", d), part_in.at[d - 1])
-        value[...] += part_in[d - 1].astype(F32)
+        to = (q + d) % 4
+        send(("gate", d), gate.at[:, quarter(to)], gt.at[q], at(x, y, to), h)
+
+    def product(d):
+        i = ORDER.index(d)
+        spread_end(i, 1)
+        return jnp.dot(
+            tok[...].reshape(BLOCK, FEAT), wf[chunks[i]].reshape(FEAT, LANE), preferred_element_type=F32
+        )
+
+    half = BLOCK // 2
+    low, high = pl.ds(0, half), pl.ds(half, half)
+
+    def give(name, slot, rows, to, ch):
+        send(name, part_out.at[slot, rows, :], to, ctx, ch)
+
+    up, down = (h + 1) % 4, (h + 3) % 4
+    part_out[2] = product(2).astype(BF16)
+    give("hop up", 2, low, passed.at[0], up)
+    give("hop down", 2, high, passed.at[1], down)
+    total = product(1)
+    conv[low, :] = total[:half]
+    part_out[0, high, :] = total[half:].astype(BF16)
+    give("up high", 0, high, part_in.at[0, high, :], up)
+    total = product(3)
+    conv[high, :] = total[half:]
+    part_out[1, low, :] = total[:half].astype(BF16)
+    give("down low", 1, low, part_in.at[1, low, :], down)
+    arrive("hop up", passed.at[0])
+    part_out[0, low, :] = (conv[low, :] + passed[0].astype(F32)).astype(BF16)
+    give("up low", 0, low, part_in.at[0, low, :], up)
+    arrive("hop down", passed.at[1])
+    part_out[1, high, :] = (conv[high, :] + passed[1].astype(F32)).astype(BF16)
+    give("down high", 1, high, part_in.at[1, high, :], down)
+    value[...] = product(0)
+    arrive("up high", part_in.at[0, high, :])
+    arrive("down low", part_in.at[1, low, :])
+    arrive("up low", part_in.at[0, low, :])
+    arrive("down high", part_in.at[1, high, :])
+    value[...] += part_in[0].astype(F32) + part_in[1].astype(F32)
     value[...] = value[...].astype(BF16).astype(F32)
 
     run_states(value, runs, pre, pim, sre, sim)
@@ -327,26 +373,39 @@
         total = conv[here, :] + skip_v[...] * value[here, :]
         mixed[here, :] = (gt[j].astype(F32) * total).astype(BF16)
 
-    own = None
-    for dh in (2, 1, 3, 0):
+    half = ROWS // 2
+
+    def part(i):
+        return pl.ds(i * half, half)
+
+    def give_mixed(dh, i):
         for dq in range(N):
             to = (q + dq) % 4
-            src = mixed.at[pl.ds(pl.multiple_of(to * ROWS, ROWS), ROWS), :]
-            dst = seen.at[h, :, quarter(q)]
-            if dh == 0 and dq == 0:
-                own = pltpu.make_async_copy(src, dst, loc.at[7])
-                own.start()
-            else:
-                send(("mixed", dh, dq), src, dst, at(x, y, to), (h + dh) % 4)
-    local[6].wait()
-    for step, dh in enumerate((0, 1, 3, 2)):
-        source = (h + 4 - dh) % 4
+            src = mixed.at[pl.ds(pl.multiple_of(to * ROWS + i * half, half), half), :]
+            send(("mixed", dh, i, dq), src, seen.at[h, part(i), quarter(q)], at(x, y, to), (h + dh) % 4)
+
+    def mixed_end(dh, i):
         for dq in range(N):
-            if dh == 0 and dq == 0:
-                own.wait()
-            else:
-                arrive(("mixed", dh, dq), seen.at[source, :, quarter((q + 4 - dq) % 4)])
-
+            dst = seen.at[(h + 4 - dh) % 4, part(i), quarter((q + 4 - dq) % 4)]
+            arrive(("mixed", dh, i, dq), dst)
+
+    def whole(to):
+        return mixed.at[pl.ds(pl.multiple_of(to * ROWS, ROWS), ROWS), :]
+
+    give_mixed(1, 0)
+    give_mixed(3, 1)
+    own = pltpu.make_async_copy(whole(q), seen.at[h, :, quarter(q)], loc.at[7])
+    own.start()
+    for dq in range(N):
+        sent(("mixed", 1, 0, dq))
+        sent(("mixed", 3, 1, dq))
+    for dq in range(1, N):
+        to = (q + dq) % 4
+        send(("mixed", dq), whole(to), seen.at[h, :, quarter(q)], at(x, y, to), h)
+    give_mixed(1, 1)
+    give_mixed(3, 0)
+
+    def project(source, step):
         def columns(n, _):
             cols = pl.ds(pl.multiple_of(n * 512, 512), 512)
             deep = pl.ds(pl.multiple_of(source * CH, CH), CH)
@@ -361,8 +420,30 @@
 
         lax.fori_loop(0, FEAT // 512, columns, 0)
 
-    for copy in sends:
+    mixed_end(1, 0)
+    src = seen.at[down, part(0), :]
+    send("pass up", src, src, ctx, up)
+    mixed_end(3, 1)
+    src = seen.at[up, part(1), :]
+    send("pass down", src, src, ctx, down)
+    local[6].wait()
+    own.wait()
+    for dq in range(1, N):
+        arrive(("mixed", dq), seen.at[h, :, quarter((q + 4 - dq) % 4)])
+    project(h, 0)
+    mixed_end(1, 1)
+    project(down, 1)
+    mixed_end(3, 0)
+    project(up, 2)
+    opposite = (h + 2) % 4
+    arrive("pass up", seen.at[opposite, part(0), :])
+    arrive("pass down", seen.at[opposite, part(1), :])
+    project(opposite, 3)
+
+    for copy in sends.values():
         copy.wait_send()
+    for away, copy in onward:
+        pl.when(away)(copy.wait_send)
     assert len(names) <= SEMS
 
 
@@ -381,7 +462,8 @@
             vmem((1, LANE), F32),
             vmem((N * CH, FEAT), BF16),
             vmem((N - 1, BLOCK, LANE), BF16),
-            vmem((N - 1, BLOCK, LANE), BF16),
+            vmem((2, BLOCK, LANE), BF16),
+            vmem((2, BLOCK // 2, LANE), BF16),
             vmem((BLOCK, LANE), F32),
             vmem((BLOCK, LANE), F32),
             vmem((2 * RUN, RUNS, LANE), F32),

time: 76.5 us -> 71.4 us (0.933)
  Pallas kernels: 74.5 us -> 69.4 us
    pallas_call x1, Pallas kernels: 74.5 us -> 69.4 us  [on_device(): pl.pallas_call(kernel, out_shape=jax.ShapeDtypeStruct((ROWS, FEAT), BF16)...]
where the time goes in v3:
time: 71.4 us; the launch traced here: 71.2 us
  Pallas kernels  69.4 us (97%)
  local copies, waits for them, and re-layouts  1.88 us (3%)
    pallas_call x1, Pallas kernels, on_device(): pl.pallas_call(kernel, out_shape=jax.ShapeDtypeStruct((ROWS, FEAT), BF16)...  69.4 us
    unnamed x1, local copies, waits for them, and re-layouts  1.88 us

profile of v3, /device:TPU:1, one launch (start us, length us, event | category | flops | bytes accessed | tf_op | source)
XLA Modules:
  0.0 71.2 jit_solution(984390590644708422)
XLA Ops:
  0.0 69.4 %shard_map.82 = bf16[128,2048]{1,0:T(8,128)(2,1)} custom-call(bf16[128,2048]{1,0:T(8,128)(2,1)} %tokens.1, bf16[128,512]{1,0:T(8,128)(2,1)} %weight.1, bf16[128,512]{1,0:T(8,128)(2,1)} %gate.1, f32[16,512]{1,0:T(8,128)} %decay.1, f32[16,512]{1,0:T(8,128)} %freq.1, f32[16,512]{1,0:T(8,128)} %residue.1, f32[1,512]{1,0:T(1,128)} %bitcast.1, ...), custom_call_target="tpu_custom_call" | custom-call | tf_op jit(solution)/shard_map/pallas_call | solution.py:452
  69.4 1.9 %copy.10 = bf16[128,2048]{1,0:T(8,128)(2,1)} copy(bf16[128,2048]{1,0:T(8,128)(2,1)} %shard_map.82) | data formatting | bytes 1048576

commit v4 on v3

--- a/solution.py
+++ b/solution.py
@@ -18,6 +18,7 @@
 BLOCK = 512
 RUN = 32
 RUNS = BLOCK // RUN
+HALF = RUNS // 2
 MODES = 16
 SPAN = 8192.0
 PIECES = 4
@@ -53,31 +54,33 @@
     filt[...] = lax.fori_loop(0, MODES, mode, jnp.zeros((RUN, LANE), F32))
 
 
-def run_states(value, runs, pre, pim, sre, sim):
-    runs[0:RUN] = jnp.zeros((RUN, RUNS, LANE), F32)
+def run_states(first, value, runs, pre, pim, sre, sim):
+    first = pl.multiple_of(first, HALF)
+    some = pl.ds(first, HALF)
 
     def split(t, _):
-        runs[RUN + t] = value[pl.ds(t, RUNS, stride=RUN), :]
+        runs[t, some, :] = jnp.zeros((HALF, LANE), F32)
+        runs[RUN + t, some, :] = value[pl.ds(first * RUN + t, HALF, stride=RUN), :]
         return 0
 
     lax.fori_loop(0, RUN, split, 0)
 
-    def modes(pair, _):
-        zero = jnp.zeros((RUNS, LANE), F32)
-        sums = [zero] * 4
+    def modes(step, _):
+        zero = jnp.zeros((HALF, LANE), F32)
+        sums = [zero] * 8
         for t in range(RUN):
-            v = runs[RUN + t]
-            for i in range(2):
-                m = pair * 2 + i
+            v = runs[RUN + t, some, :]
+            for i in range(4):
+                m = step * 4 + i
                 sums[2 * i] += pre[m, RUN - 1 - t : RUN - t, :] * v
                 sums[2 * i + 1] += pim[m, RUN - 1 - t : RUN - t, :] * v
-        for i in range(2):
-            rows = pl.ds(pl.multiple_of((pair * 2 + i) * RUNS, RUNS), RUNS)
+        for i in range(4):
+            rows = pl.ds(pl.multiple_of((step * 4 + i) * RUNS + first, HALF), HALF)
             sre[rows, :] = sums[2 * i]
             sim[rows, :] = sums[2 * i + 1]
         return 0
 
-    lax.fori_loop(0, MODES // 2, modes, 0)
+    lax.fori_loop(0, MODES // 4, modes, 0)
 
 
 def scan_runs(sre, sim, lev, carry, cre=None, cim=None):
@@ -140,7 +143,7 @@
 
 def kernel(
     tokens, weight, gate, decay, freq, residue, skip, out_weight, out,
-    tok, wf, gt, par, skip_v, ow, part_out, part_in, passed, value, conv, runs, near, rate, pre, pim, filt, lev,
+    tok, wf, gt, par, skip_v, ow, part_out, part_in, passed, held, value, conv, runs, near, rate, pre, pim, filt, lev,
     sre, sim, cre, cim, states, mixed, seen, acc, lifted, loc, sent_sem, got_sem,
 ):
     ctx = lax.axis_index("ctx")
@@ -196,11 +199,18 @@
         greet(at(x, y, (q + d) % 4), (h + d // 4) % 4)
     pl.semaphore_wait(barrier, 2 * (N * N - 1))
 
+    def give_tokens(i):
+        rows = pl.ds(i * BAND, BAND)
+        send(("across", i), tokens.at[rows, :], tok.at[q, rows, :], at(x, y, across), h)
+
     for d in (2, 1, 3):
         to = (x + d) % 4
         send(("lift", d), weight.at[band(to), :], lifted.at[x], at(to, y, q), h)
     keep = pltpu.make_async_copy(weight.at[band(x), :], lifted.at[x], loc.at[8])
     keep.start()
+
+    give_tokens(0)
+    send("beside", tokens, tok.at[q], at(x, y, beside), h)
 
     local = [
         (decay.at[:, quarter(q)], par.at[0]),
@@ -238,11 +248,8 @@
                 copy.start()
                 sends["weight", d, dq] = copy
 
-    width = FEAT // PIECES
-    for i in range(PIECES):
-        cols = pl.ds(i * width, width)
-        send(("across", i), tokens.at[:, cols], tok.at[q, :, cols], at(x, y, across), h)
-    send("beside", tokens, tok.at[q], at(x, y, beside), h)
+    for i in range(1, PIECES):
+        give_tokens(i)
 
     def weight_end(d):
         for dq in range(N):
@@ -264,6 +271,7 @@
         return wf.at[chunk, :, some, band(x), :], along_x, wf.at[chunk, :, some, band(back_x), :]
 
     chunks = [(h + d) % 4 for d in ORDER]
+
     ways = [(g, d) for d in (2, 1, 3) for g in range(2)]
 
     def spread(i, stage):
@@ -280,89 +288,122 @@
             sent(("spread", i, g, 1, d))
 
     def forward(i):
-        piece = tok.at[across, :, pl.ds(i * width, width)]
-        arrive(("across", i), piece)
-        send(("along", i), piece, piece, at(x, y, beside), h)
+        rows = pl.ds(i * BAND, BAND)
+        arrive(("across", i), tok.at[across, rows, :])
+        send(("along", i), tok.at[across, rows, :], tok.at[across, rows, :], at(x, y, beside), h)
+
+    up, down = (h + 1) % 4, (h + 3) % 4
+
+    def pair(p):
+        return (q // 2 + p) % 2 * 2
+
+    def product(d, p):
+        rows = tok[pl.ds(pair(p), 2)].reshape(2 * ROWS, FEAT)
+        columns = wf[chunks[ORDER.index(d)]].reshape(FEAT, LANE)
+        return jnp.dot(rows, columns, preferred_element_type=F32)
+
+    def give(name, src, dst, ch):
+        send(name, src, dst, ctx, ch)
+
+    def far_sums(p):
+        a, b = pair(p), pair(p) + 1
+        total = product(2, p).astype(BF16)
+        part_out[2, a], part_out[2, b] = total[:ROWS], total[ROWS:]
+        give(("hop up", p), part_out.at[2, a], passed.at[0, p], up)
+        give(("hop down", p), part_out.at[2, b], passed.at[1, p], down)
+
+    def up_sums(p):
+        a, b = pair(p), pair(p) + 1
+        total = product(1, p)
+        held[0, p] = total[:ROWS]
+        part_out[0, b] = total[ROWS:].astype(BF16)
+        give(("up b", p), part_out.at[0, b], part_in.at[0, b], up)
+
+    def down_sums(p):
+        a, b = pair(p), pair(p) + 1
+        total = product(3, p)
+        held[1, p] = total[ROWS:]
+        part_out[1, a] = total[:ROWS].astype(BF16)
+        give(("down a", p), part_out.at[1, a], part_in.at[1, a], down)
+
+    def joint_sums(p):
+        a, b = pair(p), pair(p) + 1
+        arrive(("hop up", p), passed.at[0, p])
+        part_out[0, a] = (held[0, p] + passed[0, p].astype(F32)).astype(BF16)
+        give(("up a", p), part_out.at[0, a], part_in.at[0, a], up)
+        arrive(("hop down", p), passed.at[1, p])
+        part_out[1, b] = (held[1, p] + passed[1, p].astype(F32)).astype(BF16)
+        give(("down b", p), part_out.at[1, b], part_in.at[1, b], down)
+
+    def own_sums(p):
+        value[pl.ds(pl.multiple_of(pair(p) * ROWS, 2 * ROWS), 2 * ROWS), :] = product(0, p)
+
+    def add_sums(p):
+        a, b = pair(p), pair(p) + 1
+        arrive(("up b", p), part_in.at[0, b])
+        arrive(("down a", p), part_in.at[1, a])
+        arrive(("up a", p), part_in.at[0, a])
+        arrive(("down b", p), part_in.at[1, b])
+        for i in (a, b):
+            rows = pl.ds(pl.multiple_of(i * ROWS, ROWS), ROWS)
+            total = value[rows, :] + (part_in[0, i].astype(F32) + part_in[1, i].astype(F32))
+            value[rows, :] = total.astype(BF16).astype(F32)
 
     for d in (0, 1, 3, 2):
         weight_end(d)
         spread(ORDER.index(d), 0)
-    for i in (0, 1):
-        spread_end(i, 0)
-        spread(i, 1)
     for copy in local[:3]:
         copy.wait()
     make_tables(par, rate, pre, pim, filt, lev)
-    forward(0)
-    forward(1)
-    spread_sent(0)
-    spread_end(2, 0)
-    spread(2, 1)
-    forward(2)
-    spread_sent(1)
-    spread_end(3, 0)
-    spread(3, 1)
-    forward(3)
-    arrive("beside", tok.at[beside])
-    for i in range(PIECES):
-        arrive(("along", i), tok.at[(beside + 2) % 4, :, pl.ds(i * width, width)])
-    for copy in local[3:6]:
-        copy.wait()
-
+    for i in range(N):
+        spread_end(i, 0)
+        spread(i, 1)
     for d in range(1, N):
         to = (q + d) % 4
         send(("gate", d), gate.at[:, quarter(to)], gt.at[q], at(x, y, to), h)
-
-    def product(d):
-        i = ORDER.index(d)
-        spread_end(i, 1)
-        return jnp.dot(
-            tok[...].reshape(BLOCK, FEAT), wf[chunks[i]].reshape(FEAT, LANE), preferred_element_type=F32
-        )
-
-    half = BLOCK // 2
-    low, high = pl.ds(0, half), pl.ds(half, half)
-
-    def give(name, slot, rows, to, ch):
-        send(name, part_out.at[slot, rows, :], to, ctx, ch)
-
-    up, down = (h + 1) % 4, (h + 3) % 4
-    part_out[2] = product(2).astype(BF16)
-    give("hop up", 2, low, passed.at[0], up)
-    give("hop down", 2, high, passed.at[1], down)
-    total = product(1)
-    conv[low, :] = total[:half]
-    part_out[0, high, :] = total[half:].astype(BF16)
-    give("up high", 0, high, part_in.at[0, high, :], up)
-    total = product(3)
-    conv[high, :] = total[half:]
-    part_out[1, low, :] = total[:half].astype(BF16)
-    give("down low", 1, low, part_in.at[1, low, :], down)
-    arrive("hop up", passed.at[0])
-    part_out[0, low, :] = (conv[low, :] + passed[0].astype(F32)).astype(BF16)
-    give("up low", 0, low, part_in.at[0, low, :], up)
-    arrive("hop down", passed.at[1])
-    part_out[1, high, :] = (conv[high, :] + passed[1].astype(F32)).astype(BF16)
-    give("down high", 1, high, part_in.at[1, high, :], down)
-    value[...] = product(0)
-    arrive("up high", part_in.at[0, high, :])
-    arrive("down low", part_in.at[1, low, :])
-    arrive("up low", part_in.at[0, low, :])
-    arrive("down high", part_in.at[1, high, :])
-    value[...] += part_in[0].astype(F32) + part_in[1].astype(F32)
-    value[...] = value[...].astype(BF16).astype(F32)
-
-    run_states(value, runs, pre, pim, sre, sim)
+    for i in range(PIECES):
+        forward(i)
+    for copy in local[3:6]:
+        copy.wait()
+    arrive("beside", tok.at[beside])
+    spread_end(0, 1)
+    far_sums(0)
+    spread_end(1, 1)
+    up_sums(0)
+    for i in range(PIECES):
+        arrive(("along", i), tok.at[(beside + 2) % 4, pl.ds(i * BAND, BAND), :])
+    far_sums(1)
+    up_sums(1)
+    spread_end(2, 1)
+    down_sums(0)
+    down_sums(1)
+    joint_sums(0)
+    joint_sums(1)
+    spread_end(3, 1)
+    own_sums(0)
+    own_sums(1)
+
+    for p in range(2):
+        add_sums(p)
+        run_states(pair(p) * ROWS // RUN, value, runs, pre, pim, sre, sim)
     zero = jnp.zeros((MODES, LANE), F32)
     end_re, end_im = scan_runs(sre, sim, lev, (zero, zero))
     states[block, 0:MODES, :] = end_re.astype(BF16)
     states[block, MODES : 2 * MODES, :] = end_im.astype(BF16)
-    for d in range(1, N * N):
-        to = (block + d) % 16
-        send(("state", d), states.at[block], states.at[block], to * 4 + q, h)
+    moves = []
+    for d in (10, 6, 9, 11, 5, 7, 8, 2, 14, 13, 3, 12, 4, 1, 15):
+        i = sem(("state", d))
+        there = (block + d) % 16
+        out_copy = remote(states.at[block], states.at[block], i, i, there * 4 + q, h)
+        back = (block + 16 - d) % 16
+        in_copy = remote(states.at[back], states.at[back], i, i, ctx, h)
+        after, before = block + d < 16, block >= d
+        pl.when(after)(out_copy.start)
+        moves.append((after, out_copy, before, in_copy))
     direct(runs, filt, near)
-    for d in range(1, N * N):
-        arrive(("state", d), states.at[(block + 16 - d) % 16])
+    for after, out_copy, before, in_copy in moves:
+        pl.when(before)(in_copy.wait_recv)
+        pl.when(after)(out_copy.wait_send)
     scan_runs(sre, sim, lev, carry_in(states, lev, block), cre, cim)
     far_part(near, pre, pim, cre, cim, conv)
 
@@ -461,9 +502,10 @@
             vmem((3, MODES, LANE), F32),
             vmem((1, LANE), F32),
             vmem((N * CH, FEAT), BF16),
-            vmem((N - 1, BLOCK, LANE), BF16),
-            vmem((2, BLOCK, LANE), BF16),
-            vmem((2, BLOCK // 2, LANE), BF16),
+            vmem((N - 1, N, ROWS, LANE), BF16),
+            vmem((2, N, ROWS, LANE), BF16),
+            vmem((2, 2, ROWS, LANE), BF16),
+            vmem((2, 2, ROWS, LANE), F32),
             vmem((BLOCK, LANE), F32),
             vmem((BLOCK, LANE), F32),
             vmem((2 * RUN, RUNS, LANE), F32),

time: 71.4 us -> 67.3 us (0.943)
  Pallas kernels: 69.4 us -> 64.6 us
    pallas_call x1, Pallas kernels: 69.4 us -> 64.6 us  [on_device(): pl.pallas_call(kernel, out_shape=jax.ShapeDtypeStruct((ROWS, FEAT), BF16)...]
where the time goes in v4:
time: 67.3 us; the launch traced here: 66.5 us
  Pallas kernels  64.6 us (96%)
  local copies, waits for them, and re-layouts  1.88 us (3%)
    pallas_call x1, Pallas kernels, on_device(): pl.pallas_call(kernel, out_shape=jax.ShapeDtypeStruct((ROWS, FEAT), BF16)...  64.6 us
    unnamed x1, local copies, waits for them, and re-layouts  1.88 us

profile of v4, /device:TPU:1, one launch (start us, length us, event | category | flops | bytes accessed | tf_op | source)
XLA Modules:
  0.0 66.5 jit_solution(2089768924587178870)
XLA Ops:
  0.0 64.6 %shard_map.82 = bf16[128,2048]{1,0:T(8,128)(2,1)} custom-call(bf16[128,2048]{1,0:T(8,128)(2,1)} %tokens.1, bf16[128,512]{1,0:T(8,128)(2,1)} %weight.1, bf16[128,512]{1,0:T(8,128)(2,1)} %gate.1, f32[16,512]{1,0:T(8,128)} %decay.1, f32[16,512]{1,0:T(8,128)} %freq.1, f32[16,512]{1,0:T(8,128)} %residue.1, f32[1,512]{1,0:T(1,128)} %bitcast.1, ...), custom_call_target="tpu_custom_call" | custom-call | tf_op jit(solution)/shard_map/pallas_call | solution.py:493
  64.6 1.9 %copy.10 = bf16[128,2048]{1,0:T(8,128)(2,1)} copy(bf16[128,2048]{1,0:T(8,128)(2,1)} %shard_map.82) | data formatting | bytes 1048576

commit v5 on v4

--- a/solution.py
+++ b/solution.py
@@ -144,7 +144,7 @@
 def kernel(
     tokens, weight, gate, decay, freq, residue, skip, out_weight, out,
     tok, wf, gt, par, skip_v, ow, part_out, part_in, passed, held, value, conv, runs, near, rate, pre, pim, filt, lev,
-    sre, sim, cre, cim, states, mixed, seen, acc, lifted, loc, sent_sem, got_sem,
+    sre, sim, cre, cim, states, mixed, seen, acc, lifted, loc, sent_sem, got_sem, ready, done,
 ):
     ctx = lax.axis_index("ctx")
     h = lax.axis_index("ch")
@@ -456,7 +456,8 @@
             if step < N - 1:
                 acc[:, cols] = total
             else:
-                out[:, cols] = total.astype(BF16)
+                ready[:, cols] = total.astype(BF16)
+                pltpu.make_async_copy(ready.at[:, cols], out.at[:, cols], done.at[n]).start()
             return 0
 
         lax.fori_loop(0, FEAT // 512, columns, 0)
@@ -480,6 +481,9 @@
     arrive("pass up", seen.at[opposite, part(0), :])
     arrive("pass down", seen.at[opposite, part(1), :])
     project(opposite, 3)
+    for n in range(FEAT // 512):
+        cols = pl.ds(n * 512, 512)
+        pltpu.make_async_copy(ready.at[:, cols], out.at[:, cols], done.at[n]).wait()
 
     for copy in sends.values():
         copy.wait_send()
@@ -494,7 +498,7 @@
         kernel,
         out_shape=jax.ShapeDtypeStruct((ROWS, FEAT), BF16),
         in_specs=[pl.BlockSpec(memory_space=pl.ANY)] * 8,
-        out_specs=pl.BlockSpec(memory_space=pltpu.VMEM),
+        out_specs=pl.BlockSpec(memory_space=pl.ANY),
         scratch_shapes=[
             vmem((N, ROWS, FEAT), BF16),
             vmem((N, N, N, ROWS, LANE), BF16),
@@ -526,6 +530,7 @@
             vmem((N, BAND, CH), BF16),
             dma((9,)),
             dma((SEMS,)), dma((SEMS,)),
+            vmem((ROWS, FEAT), BF16), dma((FEAT // 512,)),
         ],
         compiler_params=pltpu.CompilerParams(
             collective_id=0, has_side_effects=True, vmem_limit_bytes=60 * 1024 * 1024

time: 67.3 us -> 67.2 us (level)
  no operation moved by 1% of the time
where the time goes in v5:
time: 67.2 us; the launch traced here: 66.4 us
  Pallas kernels  64.5 us (96%)
  local copies, waits for them, and re-layouts  1.88 us (3%)
    pallas_call x1, Pallas kernels, on_device(): pl.pallas_call(kernel, out_shape=jax.ShapeDtypeStruct((ROWS, FEAT), BF16)...  64.5 us
    unnamed x1, local copies, waits for them, and re-layouts  1.88 us

profile of v5, /device:TPU:1, one launch (start us, length us, event | category | flops | bytes accessed | tf_op | source)
XLA Modules:
  0.0 66.4 jit_solution(17512488509507602021)
XLA Ops:
  0.0 64.5 %shard_map.82 = bf16[128,2048]{1,0:T(8,128)(2,1)} custom-call(bf16[128,2048]{1,0:T(8,128)(2,1)} %tokens.1, bf16[128,512]{1,0:T(8,128)(2,1)} %weight.1, bf16[128,512]{1,0:T(8,128)(2,1)} %gate.1, f32[16,512]{1,0:T(8,128)} %decay.1, f32[16,512]{1,0:T(8,128)} %freq.1, f32[16,512]{1,0:T(8,128)} %residue.1, f32[1,512]{1,0:T(1,128)} %bitcast.1, ...), custom_call_target="tpu_custom_call" | custom-call | tf_op jit(solution)/shard_map/pallas_call | solution.py:497
  64.5 1.9 %copy.10 = bf16[128,2048]{1,0:T(8,128)(2,1)} copy(bf16[128,2048]{1,0:T(8,128)(2,1)} %shard_map.82) | data formatting | bytes 1048576
